TPU v7x, 128 devices: a whole 4x4x4 slice. The times are simulated.
128 devices in a mesh: slab: 4 (over z_lo, core), space: 32 (over y, x, z_hi).
Axes of the slice: x: 4, y: 4, z: 4 (z_hi: 2, z_lo: 2; z = z_hi * 2 + z_lo), core: 2. Of those that a mesh axis runs over, the one named last changes fastest.
Arguments:
- forcing: float32 [8, 3, 4, 4, 4, 32768], P('slab', None, None, None, None, 'space'), may hold values from -6 to 6
- coefficient: float32 [32768], P('space'), may hold values from 1.5 to 4
- neighbours: int32 [6, 32768], P(None, 'space'), may hold values from 0 to 2048, as said below
- halo_faces: int32 [2, 16384], P(None, 'space'), may hold values from 0 to 1023, as said below
- time_block: float32 [3, 3], replicated, may hold values from -0.6 to 1.6
- space_block: float32 [4, 4], replicated, may hold values from -0.6 to 1.6
- stiffness: float32 [4, 4], replicated, may hold values from -0.6 to 0.6
- time_restrict: float32 [1, 3], replicated, may hold values from 0.5 to 1.5
- space_restrict: float32 [2, 4], replicated, may hold values from 0.5 to 1.5
- coarse_smoother: float32 [2, 2], replicated, may hold values from -0.8 to 1.8
Outputs:
- correction: float32 [8, 3, 4, 4, 4, 32768], P('slab', None, None, None, None, 'space')
Inputs may be any that keep to these rules, and one draw needn't show every extreme that they name: `neighbours`: for element e of partition p (local numbers below 1024) and face f = -x, +x, -y, +y, -z, +z in that order: a local element of p whose opposite face is the same face with the same node order, or 1024 + m for the m-th element of the left partition's rightward list (row 1 of halo_faces), or 1536 + m for the m-th element of the right partition's leftward list (row 0), or 2048 where the face lies on the domain boundary. Ghost slots appear only for the -x face (left) and the +x face (right). `halo_faces`: row 0 lists, in local numbers, the 512 elements of a partition whose -x face touches the left partition, row 1 those whose +x face touches the right partition, each once.
All inputs are finite; a program needn't handle non-finite values.
Results may differ from a plain program's by a relative error of at most 0.00027.
Values sent between devices are 32-bit elements; how exact they have to be, the bound alone decides.
A program may use at most 128 MiB of HBM per device.

v0:
```python
import functools

import jax
import jax.numpy as jnp
from jax import lax
from jax.experimental import pallas as pl
from jax.experimental.pallas import tpu as pltpu
from jax.sharding import PartitionSpec as P

PENALTY = 0.3
UPWIND = 0.5
COARSE_UPWIND = 0.6
HIGHEST = lax.Precision.HIGHEST
MESH = pl.DeviceIdType.MESH
F32 = jnp.float32
BF16 = jnp.bfloat16
ROWS = 192
TILE = 256
TERMS = 3


def split(value):
    terms = []
    for _ in range(TERMS):
        term = value.astype(BF16)
        terms.append(term)
        value = value - term.astype(F32)
    return terms


def blocks(value, rows):
    return sum(value[i * rows : (i + 1) * rows] for i in range(1, TERMS)) + value[0:rows]


def product(stack, rows, terms):
    total = None
    for i in range(TERMS - 1, -1, -1):
        out = dot(stack[0 : (TERMS - i) * rows, :], terms[i])
        for j in range(TERMS - 1 - i, -1, -1):
            piece = out[j * rows : (j + 1) * rows]
            total = piece if total is None else total + piece
    return total


def dot(a, b):
    return jnp.dot(a, b, preferred_element_type=F32)


def iotas(shape):
    return (
        lax.broadcasted_iota(jnp.int32, shape, 0),
        lax.broadcasted_iota(jnp.int32, shape, 1),
    )


def digits(index):
    return index >> 6, (index >> 4) & 3, (index >> 2) & 3, index & 3


def expand(entry, row_digit, col_digit, rows, cols):
    out = None
    for a in range(rows):
        row = None
        for b in range(cols):
            value = entry(a, b)
            row = jnp.where(col_digit == b, value, 0.0 if row is None else row)
        out = row if out is None else jnp.where(row_digit == a, row, out)
    return out


def kernel(
    n_slab,
    n_space,
    f_ref,
    c_ref,
    nb_ref,
    halo_ref,
    tb_ref,
    sb_ref,
    st_ref,
    tr_ref,
    sr_ref,
    cs_ref,
    o_ref,
    v_ref,
    w_ref,
    vt_ref,
    ft_ref,
    lhs_ref,
    hot_ref,
    pick_ref,
    ghost_hot_ref,
    kl_ref,
    j_ref,
    m3_ref,
    q_ref,
    r_ref,
    rf_ref,
    send_ref,
    recv_ref,
    prev_ref,
    send3_ref,
    recv3_ref,
    sprev3_ref,
    prev3_ref,
    offset_ref,
    coarse_ref,
    ssem,
    rsem,
    ps_sem,
    pr_sem,
    s3_sem,
    r3_sem,
    cs_sem,
    cr_sem,
):
    width = c_ref.shape[1]
    ghosts = halo_ref.shape[1]
    slab = lax.axis_index("slab")
    part = lax.axis_index("space")
    right = lax.rem(part + 1, n_space)
    left = lax.rem(part + n_space - 1, n_space)

    prev_ref[...] = jnp.zeros_like(prev_ref)
    prev3_ref[...] = jnp.zeros_like(prev3_ref)
    coarse_ref[...] = jnp.zeros_like(coarse_ref)

    barrier = pltpu.get_barrier_semaphore()
    for other in (left, right):
        pl.semaphore_signal(barrier, inc=1, device_id=(slab, other), device_id_type=MESH)
    for step in range(1, n_slab):
        pl.semaphore_signal(
            barrier,
            inc=1,
            device_id=(lax.rem(slab + step, n_slab), part),
            device_id_type=MESH,
        )

    def halo_copy(rnd, side, s):
        return pltpu.make_async_remote_copy(
            src_ref=send_ref.at[rnd, side, s],
            dst_ref=recv_ref.at[rnd, side, s],
            send_sem=ssem.at[rnd, side, s],
            recv_sem=rsem.at[rnd, side, s],
            device_id=(slab, (right, left)[side]),
            device_id_type=MESH,
        )

    def prev_copy(rnd):
        return pltpu.make_async_remote_copy(
            src_ref=v_ref.at[rnd, :, pl.ds(ROWS + 128, 64)],
            dst_ref=prev_ref.at[rnd],
            send_sem=ps_sem.at[rnd],
            recv_sem=pr_sem.at[rnd],
            device_id=(lax.rem(slab + 1, n_slab), part),
            device_id_type=MESH,
        )

    def halo3_copy(side):
        return pltpu.make_async_remote_copy(
            src_ref=send3_ref.at[side],
            dst_ref=recv3_ref.at[side],
            send_sem=s3_sem.at[side],
            recv_sem=r3_sem.at[side],
            device_id=(slab, (right, left)[side]),
            device_id_type=MESH,
        )

    prev3_copy = pltpu.make_async_remote_copy(
        src_ref=sprev3_ref,
        dst_ref=prev3_ref,
        send_sem=ps_sem.at[2],
        recv_sem=pr_sem.at[2],
        device_id=(lax.rem(slab + 1, n_slab), part),
        device_id_type=MESH,
    )

    def coarse_copy(step):
        return pltpu.make_async_remote_copy(
            src_ref=offset_ref,
            dst_ref=coarse_ref.at[step - 1],
            send_sem=cs_sem.at[step - 1],
            recv_sem=cr_sem.at[step - 1],
            device_id=(lax.rem(slab + step, n_slab), part),
            device_id_type=MESH,
        )

    coef = c_ref[...]
    inverse = 1.0 / coef

    def build_pick(k, carry):
        base = k * 64
        row = lax.broadcasted_iota(jnp.int32, (64, ghosts), 0) + base
        for side in range(2):
            listed = halo_ref[1 - side : 2 - side, :]
            pick_ref[side, pl.ds(pl.multiple_of(base, 64), 64), :] = jnp.where(
                row == listed, 1.0, 0.0
            ).astype(BF16)
        return carry

    lax.fori_loop(0, width // 64, build_pick, 0)

    ri, ci = iotas((ROWS, ROWS))
    rt, rx, ry, rz = digits(ri)
    ct, cx, cy, cz = digits(ci)

    def kron(time_entry, space_entry):
        out = expand(time_entry, rt, ct, 3, 3)
        for r, c in ((rx, cx), (ry, cy), (rz, cz)):
            out = out * expand(space_entry, r, c, 4, 4)
        return out

    def inverse_of(ref):
        return lambda a, b: (2.0 - ref[a, b]) if a == b else -ref[a, b]

    def plain(ref):
        return lambda a, b: ref[a, b]

    def store_terms(ref, value):
        rows = value.shape[0]
        for i, term in enumerate(split(value)):
            ref[i * rows : (i + 1) * rows, :] = term

    store_terms(j_ref, kron(inverse_of(tb_ref), inverse_of(sb_ref)))

    def columns(n):
        if isinstance(n, int):
            return pl.ds(n * TILE, TILE)
        return pl.ds(pl.multiple_of(n * TILE, TILE), TILE)

    def load(ref, rows, n):
        return jnp.concatenate([ref[2 * n, rows, :], ref[2 * n + 1, rows, :]], axis=1)

    def store(ref, rows, n, value):
        ref[2 * n, rows, :] = value[:, 0:128]
        ref[2 * n + 1, rows, :] = value[:, 128:256]

    def add(ref, rows, n, value):
        store(ref, rows, n, load(ref, rows, n) + value)

    def smooth(s, n, source, rnd_in, rnd_out):
        at = columns(n)
        rows = pl.ds(s * ROWS, ROWS)
        terms = split(load(w_ref, rows, n) if source is None else source[rows, at])
        if source is not None:
            for i, term in enumerate(terms):
                ft_ref[i, rows, at] = term
        update = product(j_ref, ROWS, terms) * inverse_at(at)
        if rnd_in is not None:
            update = update + load(v_ref.at[rnd_in], rows, n)
        store(v_ref.at[rnd_out], rows, n, update)
        for i, term in enumerate(split(update)):
            vt_ref[i, rows, at] = term

    def inverse_at(at):
        return 1.0 / c_ref[:, at]

    def picked_traces(rnd, s):
        for side in range(2):
            x = 3 * (1 - side)
            rows = [pl.ds(s * ROWS + t * 64 + x * 16, 16) for t in range(3)]
            lhs = jnp.concatenate([vt_ref[i, r, :] for i in range(TERMS) for r in rows], axis=0)
            send_ref[rnd, side, s] = blocks(dot(lhs, pick_ref[side]), 48)
            halo_copy(rnd, side, s).start()

    def loop(count, fn):
        def step(n, carry):
            fn(n)
            return carry

        lax.fori_loop(0, count, step, 0)

    tiles = width // TILE
    for s in (1, 0):
        loop(tiles, lambda n: smooth(s, n, f_ref, None, 0))
        if s == 1:
            pl.semaphore_wait(barrier, n_slab + 1)

            @pl.when(slab < n_slab - 1)
            def _():
                prev_copy(0).start()

        picked_traces(0, s)

    k_full = kron(plain(tb_ref), plain(sb_ref))
    same_t, same_x, same_y, same_z = rt == ct, rx == cx, ry == cy, rz == cz
    stiff = plain(st_ref)
    l_full = jnp.where(same_y & same_z, expand(stiff, rx, cx, 4, 4), 0.0)
    l_full = l_full + jnp.where(same_x & same_z, expand(stiff, ry, cy, 4, 4), 0.0)
    l_full = l_full + jnp.where(same_x & same_y, expand(stiff, rz, cz, 4, 4), 0.0)
    l_full = jnp.where(same_t, l_full, 0.0)
    store_terms(kl_ref, jnp.concatenate([k_full, l_full], axis=0))

    ci8, cj8 = iotas((8, ROWS))
    gx, gy, gz = ci8 >> 2, (ci8 >> 1) & 1, ci8 & 1
    jt, jx, jy, jz = digits(cj8)
    sr = plain(sr_ref)
    time_row = expand(lambda a, b: tr_ref[0, b], ci8 * 0, jt, 1, 3)
    by_dim = [expand(sr, g, j, 2, 4) for g, j in ((gx, jx), (gy, jy), (gz, jz))]
    restrict = time_row * by_dim[0] * by_dim[1] * by_dim[2]
    m3 = [
        jnp.dot(restrict, k_full, precision=HIGHEST, preferred_element_type=F32),
        jnp.dot(restrict, l_full, precision=HIGHEST, preferred_element_type=F32),
    ]
    for face in range(6):
        d, node = face // 2, face % 2 * 3
        at_face = expand(lambda a, b: sr_ref[a, node], (gx, gy, gz)[d], cj8 * 0, 2, 1)
        value = time_row * jnp.where((jx, jy, jz)[d] == 3 - node, at_face, 0.0)
        for other in range(3):
            if other != d:
                value = value * by_dim[other]
        m3.append(value)
    last = jnp.where(jt == 2, tr_ref[0, 0], 0.0) * by_dim[0] * by_dim[1] * by_dim[2]
    m3.append(last)
    m3.append(jnp.zeros((8, ROWS), F32))
    store_terms(m3_ref, jnp.concatenate(m3, axis=0))
    store_terms(r_ref, jnp.concatenate([restrict, jnp.zeros((8, ROWS), F32)], axis=0))
    rf = None
    for s in range(2):
        rows = pl.ds(s * ROWS, ROWS)
        term = product(r_ref, 16, [ft_ref[i, rows, :] for i in range(TERMS)])
        rf = term[0:8] if rf is None else rf + term[0:8]
    rf_ref[...] = rf

    def build_hot(k):
        base = k * 64
        row = lax.broadcasted_iota(jnp.int32, (64, width), 0) + base
        for face in range(6):
            hot_ref[face, pl.ds(pl.multiple_of(base, 64), 64), :] = jnp.where(
                row == nb_ref[face : face + 1, :], 1.0, 0.0
            ).astype(BF16)

    loop(width // 64, build_hot)

    def build_ghost(k):
        base = k * 64
        row = lax.broadcasted_iota(jnp.int32, (64, width), 0) + base
        for side in range(2):
            first = width + side * ghosts
            ghost_hot_ref[side, pl.ds(pl.multiple_of(base, 64), 64), :] = jnp.where(
                row + first == nb_ref[side : side + 1, :], 1.0, 0.0
            ).astype(BF16)

    loop(ghosts // 64, build_ghost)

    def residual_tile(rnd, s, n):
        at = columns(n)
        rows = pl.ds(s * ROWS, ROWS)
        c = c_ref[:, at]
        out = product(kl_ref, 2 * ROWS, [vt_ref[i, rows, at] for i in range(TERMS)])
        k_part, l_part = out[0:ROWS], out[ROWS:]
        store(w_ref, rows, n, f_ref[rows, at] - c * k_part - l_part)
        if s == 1:
            add(w_ref, pl.ds(ROWS, 64), n, UPWIND * c * load(v_ref.at[rnd], pl.ds(128, 64), n))

    def face_rows(face):
        d, node = face // 2, face % 2 * 3
        if d == 0:
            return [pl.ds(st * 64 + node * 16, 16) for st in range(6)]
        if d == 1:
            return [pl.ds(node * 4 + z, 24, stride=16) for z in range(4)]
        return [pl.ds(node, 96, stride=4)]

    def stage_traces(rnd, n):
        at = columns(n)
        for face in range(6):
            trace = jnp.concatenate([load(v_ref.at[rnd], r, n) for r in face_rows(face ^ 1)], axis=0)
            for i, term in enumerate(split(trace)):
                lhs_ref[face, i * 96 : (i + 1) * 96, at] = term

    def couple(face, n):
        at = columns(n)
        out = dot(lhs_ref[face], hot_ref[face, :, at])
        out = PENALTY * blocks(out, 96)
        first = 0
        for r in face_rows(face):
            add(w_ref, r, n, out[first : first + r.size])
            first += r.size

    def upwind(rnd, n):
        add(w_ref, pl.ds(0, 64), n, UPWIND * c_ref[:, columns(n)] * load(prev_ref.at[rnd], pl.ds(0, 64), n))

    def couple_ghosts(rnd, side, s, n):
        lhs = jnp.concatenate(split(recv_ref[rnd, side, s]), axis=0)
        out = PENALTY * blocks(dot(lhs, ghost_hot_ref[side, :, columns(n)]), 48)
        for t in range(3):
            r = pl.ds(s * ROWS + t * 64 + side * 48, 16)
            add(w_ref, r, n, out[16 * t : 16 * t + 16])

    for rnd in range(2):
        for s in range(2):
            loop(tiles, lambda n: residual_tile(rnd, s, n))
        loop(tiles, lambda n: stage_traces(rnd, n))
        for face in range(6):
            loop(tiles, lambda n: couple(face, n))
        for s in (1, 0):
            if s == 0:

                @pl.when(slab > 0)
                def _():
                    prev_copy(rnd).wait_recv()

                loop(tiles, lambda n: upwind(rnd, n))
            for side in range(2):
                halo_copy(rnd, side, s).wait_recv()
                loop(tiles, lambda n: couple_ghosts(rnd, side, s, n))
            loop(tiles, lambda n: smooth(s, n, None, rnd, rnd + 1))
            if rnd == 0:
                if s == 1:

                    @pl.when(slab < n_slab - 1)
                    def _():
                        prev_copy(1).start()

                picked_traces(1, s)

    ys = []
    for s in range(2):
        rows = pl.ds(s * ROWS, ROWS)
        ys.append(product(m3_ref, 80, [vt_ref[i, rows, :] for i in range(TERMS)]))
    sprev3_ref[...] = ys[1][64:72]

    @pl.when(slab < n_slab - 1)
    def _():
        prev3_copy.start()

    summed = ys[0] + ys[1]

    def narrow_terms(value):
        terms = [term.astype(F32) for term in split(value)]
        return jnp.concatenate(terms + [jnp.zeros_like(value)], axis=0).astype(BF16)

    for face in range(6):
        q_ref[:, pl.ds(face * width, width)] = narrow_terms(
            summed[16 + 8 * face : 24 + 8 * face]
        )
    for side in range(2):
        out = dot(q_ref[:, pl.ds(side * width, width)], pick_ref[side])
        send3_ref[side] = blocks(out, 8)
        halo3_copy(side).start()
    grouped = rf_ref[...] - summed[8:16]
    grouped = grouped + coef * (UPWIND * ys[0][64:72] - summed[0:8])
    local = None
    for face in range(6):
        term = dot(q_ref[:, pl.ds(face * width, width)], hot_ref[face])
        local = term if local is None else local + term
    for side in range(2):
        halo3_copy(side).wait_recv()
        local = local + dot(narrow_terms(recv3_ref[side]), ghost_hot_ref[side])
    grouped = grouped + PENALTY * blocks(local, 8)

    @pl.when(slab > 0)
    def _():
        prev3_copy.wait_recv()

    grouped = grouped + UPWIND * coef * prev3_ref[...]

    ai, aj = iotas((8, 8))
    cs = plain(cs_ref)
    smoother = expand(cs, ai >> 2, aj >> 2, 2, 2)
    smoother = smoother * expand(cs, (ai >> 1) & 1, (aj >> 1) & 1, 2, 2)
    smoother = smoother * expand(cs, ai & 1, aj & 1, 2, 2)
    offset = jnp.dot(smoother, grouped * inverse, precision=HIGHEST, preferred_element_type=F32)
    offset_ref[...] = offset
    for step in range(1, n_slab):

        @pl.when(slab < n_slab - step)
        def _():
            coarse_copy(step).start()

    for step in range(1, n_slab):

        @pl.when(slab >= step)
        def _():
            coarse_copy(step).wait_recv()

    state = coarse_ref[n_slab - 2]
    for step in range(n_slab - 2, -1, -1):
        term = coarse_ref[step - 1] if step else offset
        state = term + COARSE_UPWIND * jnp.dot(
            smoother, state, precision=HIGHEST, preferred_element_type=F32
        )

    pi, pk = iotas((ROWS, 8))
    pt, px, py, pz = digits(pi)
    spread = expand(lambda a, b: tr_ref[0, a], pt, pk * 0, 3, 1)
    for r, g in ((px, pk >> 2), (py, (pk >> 1) & 1), (pz, pk & 1)):
        spread = spread * expand(lambda a, b: sr_ref[b, a], r, g, 4, 2)
    lifted = jnp.dot(spread, state, precision=HIGHEST, preferred_element_type=F32)
    for s in range(2):
        rows = pl.ds(s * ROWS, ROWS)
        for n in range(tiles):
            o_ref[rows, columns(n)] = load(v_ref.at[2], rows, n) + lifted[:, n * TILE : n * TILE + TILE]

    for rnd in range(2):
        for side in range(2):
            for s in range(2):
                halo_copy(rnd, side, s).wait_send()
    for side in range(2):
        halo3_copy(side).wait_send()

    @pl.when(slab < n_slab - 1)
    def _():
        prev_copy(0).wait_send()
        prev_copy(1).wait_send()
        prev3_copy.wait_send()

    for step in range(1, n_slab):

        @pl.when(slab < n_slab - step)
        def _():
            coarse_copy(step).wait_send()


def body(
    forcing,
    coefficient,
    neighbours,
    halo_faces,
    time_block,
    space_block,
    stiffness,
    time_restrict,
    space_restrict,
    coarse_smoother,
):
    n_slab, n_space = lax.axis_size("slab"), lax.axis_size("space")
    width, ghosts = coefficient.shape[0], halo_faces.shape[1]
    field = (2 * ROWS, width)
    lanes = (width // 128, 2 * ROWS, 128)
    dma = pltpu.SemaphoreType.DMA
    vmem = pl.BlockSpec(memory_space=pltpu.VMEM)
    smem = pl.BlockSpec(memory_space=pltpu.SMEM)
    out = pl.pallas_call(
        functools.partial(kernel, n_slab, n_space),
        out_shape=jax.ShapeDtypeStruct(field, F32),
        in_specs=[vmem] * 4 + [smem] * 6,
        out_specs=vmem,
        scratch_shapes=[
            pltpu.VMEM((3,) + lanes, F32),
            pltpu.VMEM(lanes, F32),
            pltpu.VMEM((TERMS,) + field, BF16),
            pltpu.VMEM((TERMS,) + field, BF16),
            pltpu.VMEM((6, TERMS * 96, width), BF16),
            pltpu.VMEM((6, width, width), BF16),
            pltpu.VMEM((2, width, ghosts), BF16),
            pltpu.VMEM((2, ghosts, width), BF16),
            pltpu.VMEM((TERMS * 2 * ROWS, ROWS), BF16),
            pltpu.VMEM((TERMS * ROWS, ROWS), BF16),
            pltpu.VMEM((TERMS * 80, ROWS), BF16),
            pltpu.VMEM((32, 6 * width), BF16),
            pltpu.VMEM((TERMS * 16, ROWS), BF16),
            pltpu.VMEM((8, width), F32),
            pltpu.VMEM((2, 2, 2, 48, ghosts), F32),
            pltpu.VMEM((2, 2, 2, 48, ghosts), F32),
            pltpu.VMEM((2, width // 128, 64, 128), F32),
            pltpu.VMEM((2, 8, ghosts), F32),
            pltpu.VMEM((2, 8, ghosts), F32),
            pltpu.VMEM((8, width), F32),
            pltpu.VMEM((8, width), F32),
            pltpu.VMEM((8, width), F32),
            pltpu.VMEM((n_slab - 1, 8, width), F32),
            dma((2, 2, 2)),
            dma((2, 2, 2)),
            dma((3,)),
            dma((3,)),
            dma((2,)),
            dma((2,)),
            dma((n_slab - 1,)),
            dma((n_slab - 1,)),
        ],
        compiler_params=pltpu.CompilerParams(
            collective_id=0, has_side_effects=True, vmem_limit_bytes=58 * 1024 * 1024
        ),
        name="window",
    )(
        forcing.reshape(field),
        coefficient.reshape(1, width),
        neighbours,
        halo_faces,
        time_block,
        space_block,
        stiffness,
        time_restrict,
        space_restrict,
        coarse_smoother,
    )
    return out.reshape(forcing.shape)


def solution(mesh):
    in_specs = (
        P("slab", None, None, None, None, "space"),
        P("space"),
        P(None, "space"),
        P(None, "space"),
        P(),
        P(),
        P(),
        P(),
        P(),
        P(),
    )
    out_specs = P("slab", None, None, None, None, "space")
    return jax.shard_map(body, mesh=mesh, in_specs=in_specs, out_specs=out_specs, check_vma=False)
```

profile of v0, /device:TPU:1, one launch (start us, length us, event | category | flops | bytes accessed | tf_op | source)
XLA Modules:
  0.0 71.5 jit_solution(3201941714467696849)
XLA Ops:
  0.0 2.7 %reshape.9.f_ref = f32[384,1024]{1,0:T(8,128)} reshape(f32[2,3,4,4,4,1024]{5,4,3,2,1,0:T(4,128)} %param.10) | data formatting | bytes 3145728 | tf_op jit(solution)/shard_map/reshape | solution.py:577
  2.7 66.0 %window.1 = f32[384,1024]{1,0:T(8,128)} custom-call(f32[384,1024]{1,0:T(8,128)} %reshape.9.f_ref, f32[1,1024]{1,0:T(1,128)} %bitcast.1, s32[6,1024]{1,0:T(8,128)} %nb_ref.1, s32[2,512]{1,0:T(2,128)} %halo_ref.1, f32[3,3]{1,0:T(4,128)} %tb_ref.1, f32[4,4]{1,0:T(4,128)} %sb_ref.1, f32[4,4]{1,0:T(4,128)} %st_ref.1, f32[1,3]{1,0:T(1,128)} %tr_ref.1, ...), custom_call_target="tpu_custom_call" | custom-call | tf_op jit(solution)/shard_map/window/pallas_call | solution.py:534
  68.8 2.7 %reshape.11 = f32[2,3,4,4,4,1024]{5,4,3,2,1,0:T(4,128)} reshape(f32[384,1024]{1,0:T(8,128)} %window.1) | data formatting | bytes 3145728 | tf_op jit(solution)/shard_map/reshape | solution.py:588
where the time goes:
time: 71.8 us; the launch traced here: 71.5 us
  Pallas kernels  66 us (92%)
  local copies, waits for them, and re-layouts  5.43 us (8%)
    pallas_call x1, Pallas kernels, body(): pl.pallas_call(functools.partial(kernel, n_slab, n_space), out_shape=jax....  66 us
    reshape x1, local copies, waits for them, and re-layouts, body(): forcing.reshape(field)  2.73 us
    reshape x1, local copies, waits for them, and re-layouts, body(): return out.reshape(forcing.shape)  2.7 us

commit v1 on v0

--- a/solution.py
+++ b/solution.py
@@ -238,6 +238,10 @@
     def add(ref, rows, n, value):
         store(ref, rows, n, load(ref, rows, n) + value)
 
+    def add_wide(ref, rows, value):
+        for n in range(width // TILE):
+            add(ref, rows, n, value[:, n * TILE : (n + 1) * TILE])
+
     def smooth(s, n, source, rnd_in, rnd_out):
         at = columns(n)
         rows = pl.ds(s * ROWS, ROWS)
@@ -263,6 +267,10 @@
             send_ref[rnd, side, s] = blocks(dot(lhs, pick_ref[side]), 48)
             halo_copy(rnd, side, s).start()
 
+    def tiled(fn):
+        for n in range(width // TILE):
+            fn(n)
+
     def loop(count, fn):
         def step(n, carry):
             fn(n)
@@ -272,7 +280,7 @@
 
     tiles = width // TILE
     for s in (1, 0):
-        loop(tiles, lambda n: smooth(s, n, f_ref, None, 0))
+        tiled(lambda n: smooth(s, n, f_ref, None, 0))
         if s == 1:
             pl.semaphore_wait(barrier, n_slab + 1)
 
@@ -368,31 +376,29 @@
             for i, term in enumerate(split(trace)):
                 lhs_ref[face, i * 96 : (i + 1) * 96, at] = term
 
-    def couple(face, n):
-        at = columns(n)
-        out = dot(lhs_ref[face], hot_ref[face, :, at])
-        out = PENALTY * blocks(out, 96)
+    def couple(face):
+        out = PENALTY * blocks(dot(lhs_ref[face], hot_ref[face]), 96)
         first = 0
         for r in face_rows(face):
-            add(w_ref, r, n, out[first : first + r.size])
+            add_wide(w_ref, r, out[first : first + r.size])
             first += r.size
 
     def upwind(rnd, n):
         add(w_ref, pl.ds(0, 64), n, UPWIND * c_ref[:, columns(n)] * load(prev_ref.at[rnd], pl.ds(0, 64), n))
 
-    def couple_ghosts(rnd, side, s, n):
+    def couple_ghosts(rnd, side, s):
         lhs = jnp.concatenate(split(recv_ref[rnd, side, s]), axis=0)
-        out = PENALTY * blocks(dot(lhs, ghost_hot_ref[side, :, columns(n)]), 48)
+        out = PENALTY * blocks(dot(lhs, ghost_hot_ref[side]), 48)
         for t in range(3):
             r = pl.ds(s * ROWS + t * 64 + side * 48, 16)
-            add(w_ref, r, n, out[16 * t : 16 * t + 16])
+            add_wide(w_ref, r, out[16 * t : 16 * t + 16])
 
     for rnd in range(2):
         for s in range(2):
-            loop(tiles, lambda n: residual_tile(rnd, s, n))
-        loop(tiles, lambda n: stage_traces(rnd, n))
+            tiled(lambda n: residual_tile(rnd, s, n))
+        tiled(lambda n: stage_traces(rnd, n))
         for face in range(6):
-            loop(tiles, lambda n: couple(face, n))
+            couple(face)
         for s in (1, 0):
             if s == 0:
 
@@ -400,11 +406,11 @@
                 def _():
                     prev_copy(rnd).wait_recv()
 
-                loop(tiles, lambda n: upwind(rnd, n))
+                tiled(lambda n: upwind(rnd, n))
             for side in range(2):
                 halo_copy(rnd, side, s).wait_recv()
-                loop(tiles, lambda n: couple_ghosts(rnd, side, s, n))
-            loop(tiles, lambda n: smooth(s, n, None, rnd, rnd + 1))
+                couple_ghosts(rnd, side, s)
+            tiled(lambda n: smooth(s, n, None, rnd, rnd + 1))
             if rnd == 0:
                 if s == 1:
 

time: 71.8 us -> 54.7 us (0.76)
  Pallas kernels: 66 us -> 48.5 us
    pallas_call x1, Pallas kernels: 66 us -> 48.5 us  [body(): pl.pallas_call(functools.partial(kernel, n_slab, n_space), out_shape=jax....]
where the time goes in v1:
time: 54.7 us; the launch traced here: 54 us
  Pallas kernels  48.5 us (89%)
  local copies, waits for them, and re-layouts  5.43 us (10%)
    pallas_call x1, Pallas kernels, body(): pl.pallas_call(functools.partial(kernel, n_slab, n_space), out_shape=jax....  48.5 us
    reshape x1, local copies, waits for them, and re-layouts, body(): forcing.reshape(field)  2.73 us
    reshape x1, local copies, waits for them, and re-layouts, body(): return out.reshape(forcing.shape)  2.7 us

profile of v1, /device:TPU:1, one launch (start us, length us, event | category | flops | bytes accessed | tf_op | source)
XLA Modules:
  0.0 54.0 jit_solution(15481270137326357388)
XLA Ops:
  0.0 2.7 %reshape.9.f_ref = f32[384,1024]{1,0:T(8,128)} reshape(f32[2,3,4,4,4,1024]{5,4,3,2,1,0:T(4,128)} %param.10) | data formatting | bytes 3145728 | tf_op jit(solution)/shard_map/reshape | solution.py:583
  2.7 48.5 %window.1 = f32[384,1024]{1,0:T(8,128)} custom-call(f32[384,1024]{1,0:T(8,128)} %reshape.9.f_ref, f32[1,1024]{1,0:T(1,128)} %bitcast.1, s32[6,1024]{1,0:T(8,128)} %nb_ref.1, s32[2,512]{1,0:T(2,128)} %halo_ref.1, f32[3,3]{1,0:T(4,128)} %tb_ref.1, f32[4,4]{1,0:T(4,128)} %sb_ref.1, f32[4,4]{1,0:T(4,128)} %st_ref.1, f32[1,3]{1,0:T(1,128)} %tr_ref.1, ...), custom_call_target="tpu_custom_call" | custom-call | tf_op jit(solution)/shard_map/window/pallas_call | solution.py:540
  51.3 2.7 %reshape.11 = f32[2,3,4,4,4,1024]{5,4,3,2,1,0:T(4,128)} reshape(f32[384,1024]{1,0:T(8,128)} %window.1) | data formatting | bytes 3145728 | tf_op jit(solution)/shard_map/reshape | solution.py:594

commit v2 on v1

--- a/solution.py
+++ b/solution.py
@@ -17,11 +17,12 @@
 ROWS = 192
 TILE = 256
 TERMS = 3
-
-
-def split(value):
+PICKED = 2
+
+
+def split(value, count=TERMS):
     terms = []
-    for _ in range(TERMS):
+    for _ in range(count):
         term = value.astype(BF16)
         terms.append(term)
         value = value - term.astype(F32)
@@ -29,7 +30,8 @@
 
 
 def blocks(value, rows):
-    return sum(value[i * rows : (i + 1) * rows] for i in range(1, TERMS)) + value[0:rows]
+    count = value.shape[0] // rows
+    return sum(value[i * rows : (i + 1) * rows] for i in range(1, count)) + value[0:rows]
 
 
 def product(stack, rows, terms):
@@ -71,7 +73,7 @@
 def kernel(
     n_slab,
     n_space,
-    f_ref,
+    forcing_ref,
     c_ref,
     nb_ref,
     halo_ref,
@@ -81,7 +83,9 @@
     tr_ref,
     sr_ref,
     cs_ref,
-    o_ref,
+    iterate_ref,
+    state_ref,
+    f_ref,
     v_ref,
     w_ref,
     vt_ref,
@@ -113,6 +117,8 @@
     r3_sem,
     cs_sem,
     cr_sem,
+    in_sem,
+    out_sem,
 ):
     width = c_ref.shape[1]
     ghosts = halo_ref.shape[1]
@@ -120,6 +126,23 @@
     part = lax.axis_index("space")
     right = lax.rem(part + 1, n_space)
     left = lax.rem(part + n_space - 1, n_space)
+
+    def half_copy(s, h):
+        return pltpu.make_async_copy(
+            forcing_ref.at[pl.ds(s * 24, 24), h],
+            f_ref.at[pl.ds(s * 24, 24), pl.ds(4 * h, 4), :],
+            in_sem.at[s, h],
+        )
+
+    def out_copy(s):
+        rows = pl.ds(s * ROWS, ROWS)
+        return pltpu.make_async_copy(
+            v_ref.at[2, :, rows, :], iterate_ref.at[:, rows, :], out_sem.at[s]
+        )
+
+    for s in (1, 0):
+        for h in range(2):
+            half_copy(s, h).start()
 
     prev_ref[...] = jnp.zeros_like(prev_ref)
     prev3_ref[...] = jnp.zeros_like(prev3_ref)
@@ -242,10 +265,13 @@
         for n in range(width // TILE):
             add(ref, rows, n, value[:, n * TILE : (n + 1) * TILE])
 
+    def field_tile(s, at):
+        return f_ref[pl.ds(s * 24, 24), :, at].reshape(ROWS, TILE)
+
     def smooth(s, n, source, rnd_in, rnd_out):
         at = columns(n)
         rows = pl.ds(s * ROWS, ROWS)
-        terms = split(load(w_ref, rows, n) if source is None else source[rows, at])
+        terms = split(load(w_ref, rows, n) if source is None else field_tile(s, at))
         if source is not None:
             for i, term in enumerate(terms):
                 ft_ref[i, rows, at] = term
@@ -263,7 +289,7 @@
         for side in range(2):
             x = 3 * (1 - side)
             rows = [pl.ds(s * ROWS + t * 64 + x * 16, 16) for t in range(3)]
-            lhs = jnp.concatenate([vt_ref[i, r, :] for i in range(TERMS) for r in rows], axis=0)
+            lhs = jnp.concatenate([vt_ref[i, r, :] for i in range(PICKED) for r in rows], axis=0)
             send_ref[rnd, side, s] = blocks(dot(lhs, pick_ref[side]), 48)
             halo_copy(rnd, side, s).start()
 
@@ -280,6 +306,8 @@
 
     tiles = width // TILE
     for s in (1, 0):
+        for h in range(2):
+            half_copy(s, h).wait()
         tiled(lambda n: smooth(s, n, f_ref, None, 0))
         if s == 1:
             pl.semaphore_wait(barrier, n_slab + 1)
@@ -330,24 +358,29 @@
         rf = term[0:8] if rf is None else rf + term[0:8]
     rf_ref[...] = rf
 
+    numbers = lax.broadcasted_iota(jnp.int32, (64, width), 0).astype(F32).astype(BF16)
+    one, zero = jnp.ones((64, width), BF16), jnp.zeros((64, width), BF16)
+
+    def hot_rows(index):
+        index = jnp.broadcast_to(index.astype(F32), (64, width)).astype(BF16)
+        return jnp.where(numbers == index, one, zero)
+
     def build_hot(k):
         base = k * 64
-        row = lax.broadcasted_iota(jnp.int32, (64, width), 0) + base
         for face in range(6):
-            hot_ref[face, pl.ds(pl.multiple_of(base, 64), 64), :] = jnp.where(
-                row == nb_ref[face : face + 1, :], 1.0, 0.0
-            ).astype(BF16)
+            hot_ref[face, pl.ds(pl.multiple_of(base, 64), 64), :] = hot_rows(
+                nb_ref[face : face + 1, :] - base
+            )
 
     loop(width // 64, build_hot)
 
     def build_ghost(k):
         base = k * 64
-        row = lax.broadcasted_iota(jnp.int32, (64, width), 0) + base
         for side in range(2):
             first = width + side * ghosts
-            ghost_hot_ref[side, pl.ds(pl.multiple_of(base, 64), 64), :] = jnp.where(
-                row + first == nb_ref[side : side + 1, :], 1.0, 0.0
-            ).astype(BF16)
+            ghost_hot_ref[side, pl.ds(pl.multiple_of(base, 64), 64), :] = hot_rows(
+                nb_ref[side : side + 1, :] - (base + first)
+            )
 
     loop(ghosts // 64, build_ghost)
 
@@ -357,7 +390,7 @@
         c = c_ref[:, at]
         out = product(kl_ref, 2 * ROWS, [vt_ref[i, rows, at] for i in range(TERMS)])
         k_part, l_part = out[0:ROWS], out[ROWS:]
-        store(w_ref, rows, n, f_ref[rows, at] - c * k_part - l_part)
+        store(w_ref, rows, n, field_tile(s, at) - c * k_part - l_part)
         if s == 1:
             add(w_ref, pl.ds(ROWS, 64), n, UPWIND * c * load(v_ref.at[rnd], pl.ds(128, 64), n))
 
@@ -373,7 +406,7 @@
         at = columns(n)
         for face in range(6):
             trace = jnp.concatenate([load(v_ref.at[rnd], r, n) for r in face_rows(face ^ 1)], axis=0)
-            for i, term in enumerate(split(trace)):
+            for i, term in enumerate(split(trace, PICKED)):
                 lhs_ref[face, i * 96 : (i + 1) * 96, at] = term
 
     def couple(face):
@@ -387,7 +420,7 @@
         add(w_ref, pl.ds(0, 64), n, UPWIND * c_ref[:, columns(n)] * load(prev_ref.at[rnd], pl.ds(0, 64), n))
 
     def couple_ghosts(rnd, side, s):
-        lhs = jnp.concatenate(split(recv_ref[rnd, side, s]), axis=0)
+        lhs = jnp.concatenate(split(recv_ref[rnd, side, s], PICKED), axis=0)
         out = PENALTY * blocks(dot(lhs, ghost_hot_ref[side]), 48)
         for t in range(3):
             r = pl.ds(s * ROWS + t * 64 + side * 48, 16)
@@ -419,6 +452,8 @@
                         prev_copy(1).start()
 
                 picked_traces(1, s)
+            else:
+                out_copy(s).start()
 
     ys = []
     for s in range(2):
@@ -442,7 +477,7 @@
         )
     for side in range(2):
         out = dot(q_ref[:, pl.ds(side * width, width)], pick_ref[side])
-        send3_ref[side] = blocks(out, 8)
+        send3_ref[side] = blocks(out[0:24], 8)
         halo3_copy(side).start()
     grouped = rf_ref[...] - summed[8:16]
     grouped = grouped + coef * (UPWIND * ys[0][64:72] - summed[0:8])
@@ -453,7 +488,7 @@
     for side in range(2):
         halo3_copy(side).wait_recv()
         local = local + dot(narrow_terms(recv3_ref[side]), ghost_hot_ref[side])
-    grouped = grouped + PENALTY * blocks(local, 8)
+    grouped = grouped + PENALTY * blocks(local[0:24], 8)
 
     @pl.when(slab > 0)
     def _():
@@ -487,17 +522,10 @@
             smoother, state, precision=HIGHEST, preferred_element_type=F32
         )
 
-    pi, pk = iotas((ROWS, 8))
-    pt, px, py, pz = digits(pi)
-    spread = expand(lambda a, b: tr_ref[0, a], pt, pk * 0, 3, 1)
-    for r, g in ((px, pk >> 2), (py, (pk >> 1) & 1), (pz, pk & 1)):
-        spread = spread * expand(lambda a, b: sr_ref[b, a], r, g, 4, 2)
-    lifted = jnp.dot(spread, state, precision=HIGHEST, preferred_element_type=F32)
+    state_ref[...] = state
+
     for s in range(2):
-        rows = pl.ds(s * ROWS, ROWS)
-        for n in range(tiles):
-            o_ref[rows, columns(n)] = load(v_ref.at[2], rows, n) + lifted[:, n * TILE : n * TILE + TILE]
-
+        out_copy(s).wait()
     for rnd in range(2):
         for side in range(2):
             for s in range(2):
@@ -516,6 +544,23 @@
         @pl.when(slab < n_slab - step)
         def _():
             coarse_copy(step).wait_send()
+
+
+def correct(v_ref, state_ref, tr_ref, sr_ref, o_ref, lifted_ref):
+    @pl.when(pl.program_id(0) == 0)
+    def _():
+        pi, pk = iotas((ROWS, 8))
+        pt, px, py, pz = digits(pi)
+        spread = expand(lambda a, b: tr_ref[0, a], pt, pk * 0, 3, 1)
+        for r, g in ((px, pk >> 2), (py, (pk >> 1) & 1), (pz, pk & 1)):
+            spread = spread * expand(lambda a, b: sr_ref[b, a], r, g, 4, 2)
+        lifted_ref[...] = jnp.dot(
+            spread, state_ref[...], precision=HIGHEST, preferred_element_type=F32
+        )
+
+    for c in range(v_ref.shape[0]):
+        at = pl.ds(c * 128, 128)
+        o_ref[:, :, at] = (v_ref[c] + lifted_ref[:, at]).reshape(48, 4, 128)
 
 
 def body(
@@ -536,18 +581,23 @@
     lanes = (width // 128, 2 * ROWS, 128)
     dma = pltpu.SemaphoreType.DMA
     vmem = pl.BlockSpec(memory_space=pltpu.VMEM)
+    hbm = pl.BlockSpec(memory_space=pl.ANY)
     smem = pl.BlockSpec(memory_space=pltpu.SMEM)
-    out = pl.pallas_call(
+    iterate, state = pl.pallas_call(
         functools.partial(kernel, n_slab, n_space),
-        out_shape=jax.ShapeDtypeStruct(field, F32),
-        in_specs=[vmem] * 4 + [smem] * 6,
-        out_specs=vmem,
+        out_shape=(
+            jax.ShapeDtypeStruct(lanes, F32),
+            jax.ShapeDtypeStruct((8, width), F32),
+        ),
+        in_specs=[hbm] + [vmem] * 3 + [smem] * 6,
+        out_specs=(hbm, vmem),
         scratch_shapes=[
+            pltpu.VMEM((48, 8, width), F32),
             pltpu.VMEM((3,) + lanes, F32),
             pltpu.VMEM(lanes, F32),
             pltpu.VMEM((TERMS,) + field, BF16),
             pltpu.VMEM((TERMS,) + field, BF16),
-            pltpu.VMEM((6, TERMS * 96, width), BF16),
+            pltpu.VMEM((6, PICKED * 96, width), BF16),
             pltpu.VMEM((6, width, width), BF16),
             pltpu.VMEM((2, width, ghosts), BF16),
             pltpu.VMEM((2, ghosts, width), BF16),
@@ -574,13 +624,15 @@
             dma((2,)),
             dma((n_slab - 1,)),
             dma((n_slab - 1,)),
+            dma((2, 2)),
+            dma((2,)),
         ],
         compiler_params=pltpu.CompilerParams(
             collective_id=0, has_side_effects=True, vmem_limit_bytes=58 * 1024 * 1024
         ),
         name="window",
     )(
-        forcing.reshape(field),
+        forcing.reshape(48, 2, 4, width),
         coefficient.reshape(1, width),
         neighbours,
         halo_faces,
@@ -591,7 +643,22 @@
         space_restrict,
         coarse_smoother,
     )
-    return out.reshape(forcing.shape)
+    correction = pl.pallas_call(
+        correct,
+        out_shape=jax.ShapeDtypeStruct((96, 4, width), F32),
+        grid=(2,),
+        in_specs=[
+            pl.BlockSpec((width // 128, ROWS, 128), lambda s: (0, s, 0)),
+            pl.BlockSpec((8, width), lambda s: (0, 0)),
+            smem,
+            smem,
+        ],
+        out_specs=pl.BlockSpec((48, 4, width), lambda s: (s, 0, 0)),
+        scratch_shapes=[pltpu.VMEM((ROWS, width), F32)],
+        compiler_params=pltpu.CompilerParams(vmem_limit_bytes=60 * 1024 * 1024),
+        name="correct",
+    )(iterate, state, time_restrict, space_restrict)
+    return correction.reshape(forcing.shape)
 
 
 def solution(mesh):

time: 54.7 us -> 49.9 us (0.912)
  local copies, waits for them, and re-layouts: 5.43 us -> 0 us
  Pallas kernels: 48.5 us -> 49.7 us
    reshape x2 -> x0, local copies, waits for them, and re-layouts: 5.43 us -> none  [the longest x1 2.73 us: body(): forcing.reshape(field)]
    pallas_call x1 -> x2, Pallas kernels: 48.5 us -> 49.7 us  [the longest x1 46.3 us: body(): pl.pallas_call(functools.partial(kernel, n_slab, n_space), out_shape=(jax...]
where the time goes in v2:
time: 49.9 us; the launch traced here: 49.7 us
  Pallas kernels  49.7 us (100%)
    pallas_call x1, Pallas kernels, body(): pl.pallas_call(functools.partial(kernel, n_slab, n_space), out_shape=(jax...  46.3 us
    pallas_call x1, Pallas kernels, body(): pl.pallas_call(correct, out_shape=jax.ShapeDtypeStruct((96, 4, width), F3...  3.33 us

profile of v2, /device:TPU:1, one launch (start us, length us, event | category | flops | bytes accessed | tf_op | source)
XLA Modules:
  0.0 49.7 jit_solution(2850768275797563132)
XLA Ops:
  0.0 46.3 %window.1 = (f32[8,384,128]{2,1,0:T(8,128)}, f32[8,1024]{1,0:T(8,128)}) custom-call(f32[48,2,4,1024]{3,2,1,0:T(4,128)} %bitcast.3, f32[1,1024]{1,0:T(1,128)} %bitcast.4, s32[6,1024]{1,0:T(8,128)} %nb_ref.1, s32[2,512]{1,0:T(2,128)} %halo_ref.1, f32[3,3]{1,0:T(4,128)} %tb_ref.1, f32[4,4]{1,0:T(4,128)} %sb_ref.1, f32[4,4]{1,0:T(4,128)} %st_ref.1, ...), custom_call_target="tpu_custom_call" | custom-call | tf_op jit(solution)/shard_map/window/pallas_call | solution.py:586
  46.3 3.3 %correct.1 = f32[96,4,1024]{2,1,0:T(4,128)} custom-call(f32[8,384,128]{2,1,0:T(8,128)} %get-tuple-element.7.v_ref, f32[8,1024]{1,0:T(8,128)} %get-tuple-element.8.state_ref, f32[1,3]{1,0:T(1,128)} %tr_ref.3, f32[2,4]{1,0:T(2,128)} %sr_ref.3), custom_call_target="tpu_custom_call" | custom-call | tf_op jit(solution)/shard_map/correct/pallas_call | solution.py:646

commit v3 on v2

--- a/solution.py
+++ b/solution.py
@@ -99,7 +99,6 @@
     m3_ref,
     q_ref,
     r_ref,
-    rf_ref,
     send_ref,
     recv_ref,
     prev_ref,
@@ -211,14 +210,18 @@
     coef = c_ref[...]
     inverse = 1.0 / coef
 
+    def hot_rows(index):
+        shape = (64, index.shape[1])
+        numbers = lax.broadcasted_iota(jnp.int32, shape, 0).astype(F32).astype(BF16)
+        index = jnp.broadcast_to(index.astype(F32), shape).astype(BF16)
+        return jnp.where(numbers == index, jnp.ones(shape, BF16), jnp.zeros(shape, BF16))
+
     def build_pick(k, carry):
         base = k * 64
-        row = lax.broadcasted_iota(jnp.int32, (64, ghosts), 0) + base
         for side in range(2):
-            listed = halo_ref[1 - side : 2 - side, :]
-            pick_ref[side, pl.ds(pl.multiple_of(base, 64), 64), :] = jnp.where(
-                row == listed, 1.0, 0.0
-            ).astype(BF16)
+            pick_ref[side, pl.ds(pl.multiple_of(base, 64), 64), :] = hot_rows(
+                halo_ref[1 - side : 2 - side, :] - base
+            )
         return carry
 
     lax.fori_loop(0, width // 64, build_pick, 0)
@@ -351,19 +354,6 @@
     m3.append(jnp.zeros((8, ROWS), F32))
     store_terms(m3_ref, jnp.concatenate(m3, axis=0))
     store_terms(r_ref, jnp.concatenate([restrict, jnp.zeros((8, ROWS), F32)], axis=0))
-    rf = None
-    for s in range(2):
-        rows = pl.ds(s * ROWS, ROWS)
-        term = product(r_ref, 16, [ft_ref[i, rows, :] for i in range(TERMS)])
-        rf = term[0:8] if rf is None else rf + term[0:8]
-    rf_ref[...] = rf
-
-    numbers = lax.broadcasted_iota(jnp.int32, (64, width), 0).astype(F32).astype(BF16)
-    one, zero = jnp.ones((64, width), BF16), jnp.zeros((64, width), BF16)
-
-    def hot_rows(index):
-        index = jnp.broadcast_to(index.astype(F32), (64, width)).astype(BF16)
-        return jnp.where(numbers == index, one, zero)
 
     def build_hot(k):
         base = k * 64
@@ -426,6 +416,7 @@
             r = pl.ds(s * ROWS + t * 64 + side * 48, 16)
             add_wide(w_ref, r, out[16 * t : 16 * t + 16])
 
+    ys = {}
     for rnd in range(2):
         for s in range(2):
             tiled(lambda n: residual_tile(rnd, s, n))
@@ -454,16 +445,14 @@
                 picked_traces(1, s)
             else:
                 out_copy(s).start()
-
-    ys = []
-    for s in range(2):
-        rows = pl.ds(s * ROWS, ROWS)
-        ys.append(product(m3_ref, 80, [vt_ref[i, rows, :] for i in range(TERMS)]))
-    sprev3_ref[...] = ys[1][64:72]
-
-    @pl.when(slab < n_slab - 1)
-    def _():
-        prev3_copy.start()
+                rows = pl.ds(s * ROWS, ROWS)
+                ys[s] = product(m3_ref, 80, [vt_ref[i, rows, :] for i in range(TERMS)])
+                if s == 1:
+                    sprev3_ref[...] = ys[1][64:72]
+
+                    @pl.when(slab < n_slab - 1)
+                    def _():
+                        prev3_copy.start()
 
     summed = ys[0] + ys[1]
 
@@ -479,7 +468,12 @@
         out = dot(q_ref[:, pl.ds(side * width, width)], pick_ref[side])
         send3_ref[side] = blocks(out[0:24], 8)
         halo3_copy(side).start()
-    grouped = rf_ref[...] - summed[8:16]
+    rf = None
+    for s in range(2):
+        rows = pl.ds(s * ROWS, ROWS)
+        term = product(r_ref, 16, [ft_ref[i, rows, :] for i in range(TERMS)])
+        rf = term[0:8] if rf is None else rf + term[0:8]
+    grouped = rf - summed[8:16]
     grouped = grouped + coef * (UPWIND * ys[0][64:72] - summed[0:8])
     local = None
     for face in range(6):
@@ -546,21 +540,40 @@
             coarse_copy(step).wait_send()
 
 
-def correct(v_ref, state_ref, tr_ref, sr_ref, o_ref, lifted_ref):
-    @pl.when(pl.program_id(0) == 0)
-    def _():
-        pi, pk = iotas((ROWS, 8))
-        pt, px, py, pz = digits(pi)
-        spread = expand(lambda a, b: tr_ref[0, a], pt, pk * 0, 3, 1)
-        for r, g in ((px, pk >> 2), (py, (pk >> 1) & 1), (pz, pk & 1)):
-            spread = spread * expand(lambda a, b: sr_ref[b, a], r, g, 4, 2)
-        lifted_ref[...] = jnp.dot(
-            spread, state_ref[...], precision=HIGHEST, preferred_element_type=F32
-        )
-
-    for c in range(v_ref.shape[0]):
-        at = pl.ds(c * 128, 128)
-        o_ref[:, :, at] = (v_ref[c] + lifted_ref[:, at]).reshape(48, 4, 128)
+def correct(v_ref, coarse_ref, tr_ref, sr_ref, o_ref, state_ref, in_ref, sum_ref, state_sem, in_sem, out_sem):
+    def in_copy(s):
+        rows = pl.ds(s * ROWS, ROWS)
+        return pltpu.make_async_copy(v_ref.at[:, rows, :], in_ref.at[:, rows, :], in_sem.at[s])
+
+    def out_copy(s, h):
+        return pltpu.make_async_copy(
+            sum_ref.at[pl.ds(s * 24, 24), pl.ds(4 * h, 4), :],
+            o_ref.at[pl.ds(s * 24, 24), h],
+            out_sem.at[s, h],
+        )
+
+    state_copy = pltpu.make_async_copy(coarse_ref, state_ref, state_sem.at[0])
+    state_copy.start()
+    for s in range(2):
+        in_copy(s).start()
+    pi, pk = iotas((ROWS, 8))
+    pt, px, py, pz = digits(pi)
+    spread = expand(lambda a, b: tr_ref[0, a], pt, pk * 0, 3, 1)
+    for r, g in ((px, pk >> 2), (py, (pk >> 1) & 1), (pz, pk & 1)):
+        spread = spread * expand(lambda a, b: sr_ref[b, a], r, g, 4, 2)
+    state_copy.wait()
+    lifted = jnp.dot(spread, state_ref[...], precision=HIGHEST, preferred_element_type=F32)
+    for s in range(2):
+        in_copy(s).wait()
+        for c in range(v_ref.shape[0]):
+            at = slice(c * 128, c * 128 + 128)
+            total = in_ref[c, s * ROWS : (s + 1) * ROWS, :] + lifted[:, at]
+            sum_ref[s * 24 : (s + 1) * 24, :, at] = total.reshape(24, 8, 128)
+        for h in range(2):
+            out_copy(s, h).start()
+    for s in range(2):
+        for h in range(2):
+            out_copy(s, h).wait()
 
 
 def body(
@@ -606,7 +619,6 @@
             pltpu.VMEM((TERMS * 80, ROWS), BF16),
             pltpu.VMEM((32, 6 * width), BF16),
             pltpu.VMEM((TERMS * 16, ROWS), BF16),
-            pltpu.VMEM((8, width), F32),
             pltpu.VMEM((2, 2, 2, 48, ghosts), F32),
             pltpu.VMEM((2, 2, 2, 48, ghosts), F32),
             pltpu.VMEM((2, width // 128, 64, 128), F32),
@@ -645,16 +657,17 @@
     )
     correction = pl.pallas_call(
         correct,
-        out_shape=jax.ShapeDtypeStruct((96, 4, width), F32),
-        grid=(2,),
-        in_specs=[
-            pl.BlockSpec((width // 128, ROWS, 128), lambda s: (0, s, 0)),
-            pl.BlockSpec((8, width), lambda s: (0, 0)),
-            smem,
-            smem,
+        out_shape=jax.ShapeDtypeStruct((48, 2, 4, width), F32),
+        in_specs=[hbm, hbm, smem, smem],
+        out_specs=hbm,
+        scratch_shapes=[
+            pltpu.VMEM((8, width), F32),
+            pltpu.VMEM(lanes, F32),
+            pltpu.VMEM((48, 8, width), F32),
+            dma((1,)),
+            dma((2,)),
+            dma((2, 2)),
         ],
-        out_specs=pl.BlockSpec((48, 4, width), lambda s: (s, 0, 0)),
-        scratch_shapes=[pltpu.VMEM((ROWS, width), F32)],
         compiler_params=pltpu.CompilerParams(vmem_limit_bytes=60 * 1024 * 1024),
         name="correct",
     )(iterate, state, time_restrict, space_restrict)

time: 49.9 us -> 50.2 us (level)
  no operation moved by 1% of the time
where the time goes in v3:
time: 50.2 us; the launch traced here: 49.9 us
  Pallas kernels  49.7 us (99%)
    pallas_call x1, Pallas kernels, body(): pl.pallas_call(functools.partial(kernel, n_slab, n_space), out_shape=(jax...  46 us
    pallas_call x1, Pallas kernels, body(): pl.pallas_call(correct, out_shape=jax.ShapeDtypeStruct((48, 2, 4, width),...  3.75 us

profile of v3, /device:TPU:1, one launch (start us, length us, event | category | flops | bytes accessed | tf_op | source)
XLA Modules:
  0.0 49.9 jit_solution(16417465800330184125)
XLA Ops:
  0.0 46.0 %window.1 = (f32[8,384,128]{2,1,0:T(8,128)}, f32[8,1024]{1,0:T(8,128)}) custom-call(f32[48,2,4,1024]{3,2,1,0:T(4,128)} %bitcast.3, f32[1,1024]{1,0:T(1,128)} %bitcast.4, s32[6,1024]{1,0:T(8,128)} %nb_ref.1, s32[2,512]{1,0:T(2,128)} %halo_ref.1, f32[3,3]{1,0:T(4,128)} %tb_ref.1, f32[4,4]{1,0:T(4,128)} %sb_ref.1, f32[4,4]{1,0:T(4,128)} %st_ref.1, ...), custom_call_target="tpu_custom_call" | custom-call | tf_op jit(solution)/shard_map/window/pallas_call | solution.py:599
  46.0 3.7 %correct.1 = f32[48,2,4,1024]{3,2,1,0:T(4,128)} custom-call(f32[8,384,128]{2,1,0:T(8,128)} %get-tuple-element.7.v_ref, f32[8,1024]{1,0:T(8,128)} %get-tuple-element.8.coarse_ref, f32[1,3]{1,0:T(1,128)} %tr_ref.3, f32[2,4]{1,0:T(2,128)} %sr_ref.3), custom_call_target="tpu_custom_call" | custom-call | tf_op jit(solution)/shard_map/correct/pallas_call | solution.py:658

commit v4 on v3

--- a/solution.py
+++ b/solution.py
@@ -540,7 +540,7 @@
             coarse_copy(step).wait_send()
 
 
-def correct(v_ref, coarse_ref, tr_ref, sr_ref, o_ref, state_ref, in_ref, sum_ref, state_sem, in_sem, out_sem):
+def correct(v_ref, state_ref, tr_ref, sr_ref, o_ref, in_ref, sum_ref, in_sem, out_sem):
     def in_copy(s):
         rows = pl.ds(s * ROWS, ROWS)
         return pltpu.make_async_copy(v_ref.at[:, rows, :], in_ref.at[:, rows, :], in_sem.at[s])
@@ -552,8 +552,6 @@
             out_sem.at[s, h],
         )
 
-    state_copy = pltpu.make_async_copy(coarse_ref, state_ref, state_sem.at[0])
-    state_copy.start()
     for s in range(2):
         in_copy(s).start()
     pi, pk = iotas((ROWS, 8))
@@ -561,7 +559,6 @@
     spread = expand(lambda a, b: tr_ref[0, a], pt, pk * 0, 3, 1)
     for r, g in ((px, pk >> 2), (py, (pk >> 1) & 1), (pz, pk & 1)):
         spread = spread * expand(lambda a, b: sr_ref[b, a], r, g, 4, 2)
-    state_copy.wait()
     lifted = jnp.dot(spread, state_ref[...], precision=HIGHEST, preferred_element_type=F32)
     for s in range(2):
         in_copy(s).wait()
@@ -658,13 +655,11 @@
     correction = pl.pallas_call(
         correct,
         out_shape=jax.ShapeDtypeStruct((48, 2, 4, width), F32),
-        in_specs=[hbm, hbm, smem, smem],
+        in_specs=[hbm, vmem, smem, smem],
         out_specs=hbm,
         scratch_shapes=[
-            pltpu.VMEM((8, width), F32),
             pltpu.VMEM(lanes, F32),
             pltpu.VMEM((48, 8, width), F32),
-            dma((1,)),
             dma((2,)),
             dma((2, 2)),
         ],

time: 50.2 us -> 49.7 us (0.990)
  no operation moved by 1% of the time
where the time goes in v4:
time: 49.7 us; the launch traced here: 49.4 us
  Pallas kernels  49.3 us (99%)
    pallas_call x1, Pallas kernels, body(): pl.pallas_call(functools.partial(kernel, n_slab, n_space), out_shape=(jax...  46 us
    pallas_call x1, Pallas kernels, body(): pl.pallas_call(correct, out_shape=jax.ShapeDtypeStruct((48, 2, 4, width),...  3.26 us

profile of v4, /device:TPU:1, one launch (start us, length us, event | category | flops | bytes accessed | tf_op | source)
XLA Modules:
  0.0 49.4 jit_solution(7687639054837147270)
XLA Ops:
  0.0 46.0 %window.1 = (f32[8,384,128]{2,1,0:T(8,128)}, f32[8,1024]{1,0:T(8,128)}) custom-call(f32[48,2,4,1024]{3,2,1,0:T(4,128)} %bitcast.3, f32[1,1024]{1,0:T(1,128)} %bitcast.4, s32[6,1024]{1,0:T(8,128)} %nb_ref.1, s32[2,512]{1,0:T(2,128)} %halo_ref.1, f32[3,3]{1,0:T(4,128)} %tb_ref.1, f32[4,4]{1,0:T(4,128)} %sb_ref.1, f32[4,4]{1,0:T(4,128)} %st_ref.1, ...), custom_call_target="tpu_custom_call" | custom-call | tf_op jit(solution)/shard_map/window/pallas_call | solution.py:596
  46.0 3.3 %correct.1 = f32[48,2,4,1024]{3,2,1,0:T(4,128)} custom-call(f32[8,384,128]{2,1,0:T(8,128)} %get-tuple-element.7.v_ref, f32[8,1024]{1,0:T(8,128)} %get-tuple-element.8.state_ref, f32[1,3]{1,0:T(1,128)} %tr_ref.3, f32[2,4]{1,0:T(2,128)} %sr_ref.3), custom_call_target="tpu_custom_call" | custom-call | tf_op jit(solution)/shard_map/correct/pallas_call | solution.py:655
